TPU v7x, 512 devices: a whole 4x4x16 slice. The times are simulated.
512 devices in a mesh: section: 4 (over x), dp: 32 (over z, y_hi), mp: 4 (over y_lo, core).
Axes of the slice: x: 4, y: 4 (y_hi: 2, y_lo: 2; y = y_hi * 2 + y_lo), z: 16, core: 2. Of those that a mesh axis runs over, the one named last changes fastest.
Arguments:
- patches: bfloat16 [6144, 3200], P('dp', ('section', 'mp')), may hold values from -6 to 6
- up_first: bfloat16 [3200, 6400], P('dp', ('section', 'mp')), may hold values from -0.109375 to 0.109375
- down_first: bfloat16 [6400, 3200], P(('section', 'mp'), 'dp'), may hold values from -0.078125 to 0.078125
- up_second: bfloat16 [3200, 6400], P('dp', ('section', 'mp')), may hold values from -0.109375 to 0.109375
- down_second: bfloat16 [6400, 3200], P(('section', 'mp'), 'dp'), may hold values from -0.078125 to 0.078125
- targets: int32 [6144, 1], P('dp'), may hold values from 0 to 31; in each aligned block of 192 rows (0 to 191, 192 to 383, ...) at most 12 rows name the same one
Outputs:
- placed: bfloat16 [12288, 3200], P('dp', ('section', 'mp'))
Inputs may be any that keep to these rules, and one draw needn't show every extreme that they name: `targets`: of the rows of one block of 192, at most 12 have the same target, a bound that some block reaches.
All inputs are finite; a program needn't handle non-finite values.
Results may differ from a plain program's by a relative error of at most 0.022.
Values may be sent and summed in bfloat16 or wider, within the bound.
A program may use at most 64 MiB of HBM per device.

v0:
```python
import jax
import jax.numpy as jnp
from jax import lax
from jax.sharding import PartitionSpec as P

epsilon = 1e-06


def encoder_layer(rows, up_weight, down_weight):
    whole = lax.all_gather(rows, ("section", "mp"), axis=1, tiled=True)
    floated = whole.astype(jnp.float32)
    scale = lax.rsqrt(jnp.mean(floated * floated, axis=-1, keepdims=True) + epsilon)
    normed = (floated * scale).astype(jnp.bfloat16)
    preact = jnp.dot(
        normed,
        lax.all_gather(up_weight, "dp", axis=0, tiled=True),
        preferred_element_type=jnp.float32,
    )
    hidden = jax.nn.gelu(preact).astype(jnp.bfloat16)
    terms = jnp.dot(
        hidden,
        lax.all_gather(down_weight, "dp", axis=1, tiled=True),
        preferred_element_type=jnp.float32,
    )
    summed = lax.psum_scatter(
        terms.astype(jnp.bfloat16), ("section", "mp"), scatter_dimension=1, tiled=True
    ).astype(jnp.float32)
    return (rows.astype(jnp.float32) + summed).astype(jnp.bfloat16)


def send_rows(rows, targets):
    devices = lax.axis_size("dp")
    count = rows.shape[0]
    capacity = max(2, 2 * count // devices)
    route_list = targets[:, 0]
    onehot = (route_list[:, None] == jnp.arange(devices, dtype=jnp.int32)[None, :]).astype(
        jnp.int32
    )
    position = jnp.sum(jnp.cumsum(onehot, axis=0) * onehot, axis=1) - 1
    slots = route_list * capacity + position
    outbox = jnp.zeros((devices * capacity, rows.shape[1]), rows.dtype).at[slots].set(rows)
    arrived = lax.all_to_all(
        outbox.reshape(devices, capacity, rows.shape[1]),
        "dp",
        split_axis=0,
        concat_axis=0,
        tiled=True,
    )
    return arrived.reshape(devices * capacity, rows.shape[1])


def on_device(patches, up_first, down_first, up_second, down_second, targets):
    first = encoder_layer(patches, up_first, down_first)
    moved = send_rows(first, targets)
    return encoder_layer(moved, up_second, down_second)


def solution(mesh):
    in_specs = (
        P("dp", ("section", "mp")),
        P("dp", ("section", "mp")),
        P(("section", "mp"), "dp"),
        P("dp", ("section", "mp")),
        P(("section", "mp"), "dp"),
        P("dp", None),
    )
    out_specs = P("dp", ("section", "mp"))
    return jax.shard_map(
        on_device, mesh=mesh, in_specs=in_specs, out_specs=out_specs, check_vma=False
    )
```

profile of v0, /device:TPU:1, one launch (start us, length us, event | category | flops | bytes accessed | tf_op | source)
XLA Modules:
  0.0 905.2 jit_solution(9430548611462433292)
XLA Ops:
  6.5 0.7 all-gather.14.cloned.1.call-update
  7.3 0.0 all-gather.16.cloned.1.call-start
  7.3 0.7 all-gather.16.cloned.1.call-update
  8.0 0.0 all-gather.18.cloned.1.call-start
  8.1 0.7 all-gather.18.cloned.1.call-update
  8.7 0.0 reduce-scatter.8.cloned.1.call-start
  8.8 47.3 %all-gather.14.cloned.1.call-done = bf16[16,200,192]{1,2,0:T(8,128)(2,1)} async-done(((bf16[1,200,192]{1,2,0:T(8,128)(2,1)}), bf16[16,200,192]{1,2,0:T(8,128)(2,1)}) %all-gather.14.cloned.1.call-update) | async-done | bytes 1228816 | tf_op jit(solution)/shard_map/all_gather | solution.py:10
  56.1 4.1 copy.27
  60.2 3.5 reshape.65
  63.8 0.2 multiply_reduce_fusion
  64.0 144.0 %all-gather.16.cloned.1.call-done = bf16[32,100,400]{1,2,0:T(8,128)(2,1)} async-done(((bf16[1,100,400]{1,2,0:T(8,128)(2,1)}), bf16[32,100,400]{1,2,0:T(8,128)(2,1)}) %all-gather.16.cloned.1.call-update) | async-done | bytes 2560016 | tf_op jit(solution)/shard_map/all_gather | solution.py:16
  208.0 4.5 copy.28
  212.6 7.3 reshape.58
  219.9 144.3 %all-gather.18.cloned.1.call-done = bf16[32,100,400]{1,2,0:T(8,128)(2,1)} async-done(((bf16[1,100,400]{1,2,0:T(8,128)(2,1)}), bf16[32,100,400]{1,2,0:T(8,128)(2,1)}) %all-gather.18.cloned.1.call-update) | async-done | bytes 2560016 | tf_op jit(solution)/shard_map/all_gather | solution.py:22
  364.2 4.5 copy.29
  368.7 7.3 reshape.60
  376.0 5.5 convolution_convert_fusion.1
  381.5 2.6 copy.34
  384.2 0.0 reduce-scatter.8.cloned.1.call-update
  384.2 0.0 all-gather.20.cloned.1.call-start
  384.2 0.5 all-gather.20.cloned.1.call-update
  384.8 0.0 all-gather.22.cloned.1.call-start
  384.8 0.5 all-gather.22.cloned.1.call-update
  385.4 0.0 all-gather.12.cloned.1.call-start
  385.4 0.6 reduce-window.6
  386.0 0.2 slice_reduce_fusion
  386.3 0.1 bitcast_bitcast_fusion
  386.4 69.5 %reduce-scatter.8.cloned.1.call-done = bf16[200,192]{1,0:T(8,128)(2,1)} async-done(((bf16[3200,192]{1,0:T(8,128)(2,1)}), bf16[200,192]{1,0:T(8,128)(2,1)}) %reduce-scatter.8.cloned.1.call-update) | async-done | bytes 76816
  455.9 1.0 copy.35
  456.9 1.3 scatter_custom_fusion
  458.3 0.1 reshape.44
  458.3 31.8 %all_to_all.5 = bf16[32,12,200]{2,1,0:T(8,128)(2,1)S(1)} all-to-all(bf16[32,12,200]{2,1,0:T(8,128)(2,1)S(1)} %reshape.44), channel_id=1, replica_groups=mesh['section'=4,'dp'=32,'mp'=4] {'dp'}, dimensions={0} | all-to-all | bytes 307200 | tf_op jit(solution)/shard_map/all_to_all | solution.py:42
  490.1 0.1 reshape.45
  490.2 0.8 copy.30
  491.0 0.0 all-gather.12.cloned.1.call-update
  491.0 0.2 reduce-scatter.10.cloned.1.call-start
  491.3 119.4 %all-gather.20.cloned.1.call-done = bf16[32,100,400]{1,2,0:T(8,128)(2,1)} async-done(((bf16[1,100,400]{1,2,0:T(8,128)(2,1)}), bf16[32,100,400]{1,2,0:T(8,128)(2,1)}) %all-gather.20.cloned.1.call-update) | async-done | bytes 2560016 | tf_op jit(solution)/shard_map/all_gather | solution.py:16
  610.6 2.8 copy.32
  613.4 6.0 reshape.62
  619.4 147.7 %all-gather.22.cloned.1.call-done = bf16[32,100,400]{1,2,0:T(8,128)(2,1)} async-done(((bf16[1,100,400]{1,2,0:T(8,128)(2,1)}), bf16[32,100,400]{1,2,0:T(8,128)(2,1)}) %all-gather.22.cloned.1.call-update) | async-done | bytes 2560016 | tf_op jit(solution)/shard_map/all_gather | solution.py:22
  767.1 2.8 copy.33
  769.9 6.0 reshape.64
  775.9 40.1 %all-gather.12.cloned.1.call-done = bf16[384,3200]{0,1:T(8,128)(2,1)} async-done(((bf16[384,200]{0,1:T(8,128)(2,1)}), bf16[384,3200]{0,1:T(8,128)(2,1)}) %all-gather.12.cloned.1.call-update) | async-done | bytes 2457616 | tf_op jit(solution)/shard_map/all_gather | solution.py:10
  816.0 2.3 fusion
  818.3 8.1 convolution_convert_fusion
  826.4 0.0 reduce-scatter.10.cloned.1.call-update
  826.5 70.2 %reduce-scatter.10.cloned.1.call-done = bf16[384,200]{0,1:T(8,128)(2,1)} async-done(((bf16[384,3200]{0,1:T(8,128)(2,1)}), bf16[384,200]{0,1:T(8,128)(2,1)}) %reduce-scatter.10.cloned.1.call-update) | async-done | bytes 153616
  896.7 1.6 add_convert_fusion
  (16 shorter events, 0.1 us)
Async XLA Ops:
  6.5 49.6 %all-gather.14.cloned.1.call-start = ((), (), s32[]{:S(2)}) async-start(), calls=%async_computation.4 | async-start | bytes 1671168 | tf_op jit(solution)/shard_map/all_gather | solution.py:10
  7.3 200.8 %all-gather.16.cloned.1.call-start = ((), (), s32[]{:S(2)}) async-start(), calls=%async_computation.5 | async-start | bytes 3379200 | tf_op jit(solution)/shard_map/all_gather | solution.py:16
  8.0 356.2 %all-gather.18.cloned.1.call-start = ((), (), s32[]{:S(2)}) async-start(), calls=%async_computation.6 | async-start | bytes 3379200 | tf_op jit(solution)/shard_map/all_gather | solution.py:22
  8.7 447.2 %reduce-scatter.8.cloned.1.call-start = ((), (), s32[]{:S(2)}) async-start(), calls=%async_computation.9 | async-start | bytes 1740800
  381.5 3.9 copy-start.2
  381.5 75.4 %copy-start.1 = (bf16[192,200]{1,0:T(8,128)(2,1)S(1)}, bf16[192,200]{1,0:T(8,128)(2,1)}, u32[]{:S(2)}) copy-start(bf16[192,200]{1,0:T(8,128)(2,1)} %param.6) | copy-start | bytes 230404
  384.2 226.4 %all-gather.20.cloned.1.call-start = ((), (), s32[]{:S(2)}) async-start(), calls=%async_computation.7 | async-start | bytes 3379200 | tf_op jit(solution)/shard_map/all_gather | solution.py:16
  384.8 382.3 %all-gather.22.cloned.1.call-start = ((), (), s32[]{:S(2)}) async-start(), calls=%async_computation.8 | async-start | bytes 3379200 | tf_op jit(solution)/shard_map/all_gather | solution.py:22
  385.4 430.7 %all-gather.12.cloned.1.call-start = ((), (), s32[]{:S(2)}) async-start(), calls=%async_computation.3 | async-start | bytes 2611200 | tf_op jit(solution)/shard_map/all_gather | solution.py:10
  491.0 405.7 %reduce-scatter.10.cloned.1.call-start = ((), (), s32[]{:S(2)}) async-start(), calls=%async_computation.10 | async-start | bytes 2611200
  826.4 70.3 %copy-start = (bf16[384,200]{0,1:T(8,128)(2,1)S(1)}, bf16[384,200]{0,1:T(8,128)(2,1)}, u32[]{:S(2)}) copy-start(bf16[384,200]{0,1:T(8,128)(2,1)} %copy.30) | copy-start | bytes 460804
Sparse Core Ops, SparseCore 0:
  9.5 46.5 all-gather.13
  59.3 148.7 all-gather.15
  211.2 152.9 all-gather.17
  384.3 71.5 reduce-scatter.7
  459.4 151.1 all-gather.19
  614.1 152.9 all-gather.21
  769.5 46.5 all-gather.11
  826.6 70.0 reduce-scatter.9
where the time goes:
time: 907 us; the launch traced here: 905 us
  waiting for transfers between devices  786 us (87%)
  local copies, waits for them, and re-layouts  53.7 us (6%)
  blocking collectives  31.8 us (4%)
  matrix products  13.6 us (1%)
  between operations  13.6 us (1%)
    all_gather x2, waiting for transfers between devices, encoder_layer(): lax.all_gather(down_weight, 'dp', axis=1, tiled=True)  292 us
    all_gather x2, waiting for transfers between devices, encoder_layer(): lax.all_gather(up_weight, 'dp', axis=0, tiled=True)  263 us
    unnamed x10, waiting for transfers between devices  143 us
    all_gather x2, waiting for transfers between devices, encoder_layer(): whole = lax.all_gather(rows, ('section', 'mp'), axis=1, tiled=True)  87.5 us
    all_to_all x1, blocking collectives, send_rows(): lax.all_to_all(outbox.reshape(devices, capacity, rows.shape[1]), 'dp', sp...  31.8 us
    unnamed x12, local copies, waits for them, and re-layouts  30.4 us
  transfers between devices with their start and end apart: 8, of which 8 were waited for; matrix products, arithmetic and copies ran while one was open for 5% of the time, Pallas kernels for 0%

commit v1 on v0

v1 whole, which is shorter than its diff:
```python
import functools

import jax
import jax.numpy as jnp
from jax import lax
from jax.experimental import pallas as pl
from jax.experimental.pallas import tpu as pltpu
from jax.sharding import PartitionSpec as P

MESH = pl.DeviceIdType.MESH
EPSILON = 1e-06
DV = 3200
ROWS = 192
NZ = 16
HALF = 100
PACK = 352
CHUNKS = 2
CHUNK = PACK // CHUNKS
LANES = 256
STAGGER = 6
CAP = 12
SLOT = 16


def remote(src, dst, send, recv, device):
    return pltpu.make_async_remote_copy(
        src_ref=src, dst_ref=dst, send_sem=send, recv_sem=recv, device_id=device, device_id_type=MESH
    )


def weight_tiles(first, second):
    gap = jnp.zeros((16, 384), jnp.bfloat16)

    def wide(block):
        return jnp.concatenate([block[112 * j : 112 * j + 112] for j in range(3)], axis=1)

    main = jnp.concatenate([wide(first), gap, wide(second), gap], axis=0)
    rest = jnp.concatenate([first[336:352], second[336:352]], axis=1)
    return main, rest


def dot(a, b):
    return jnp.dot(a, b, preferred_element_type=jnp.float32)


def dot_nt(a, b):
    return lax.dot_general(a, b, (((1,), (1,)), ((), ())), preferred_element_type=jnp.float32)


def kernel(
    x_ref, w_ref, trow_ref, tcol_ref, out_ref,
    weights, xs, acc, acc_rest, squares, hid, hid_rest, staged, first_sum, staged_sum, second_sum, mine,
    pick, outbox, inbox,
    swap_send, swap_recv, ring_up_send, ring_down_send, ring_recv, sib_send, sib_recv,
    gather_send, gather_recv, one_send, one_recv, two_send, two_recv, route_send, route_recv,
):
    x, dp, mp = lax.axis_index("section"), lax.axis_index("dp"), lax.axis_index("mp")
    z, yh, yl, c = dp // 2, dp % 2, mp // 2, mp % 2
    y = yh * 2 + yl
    group = x * 4 + mp

    def at(xx, zz, yy, cc):
        return {"section": xx, "dp": zz * 2 + yy // 2, "mp": (yy % 2) * 2 + cc}

    up, down = at(x, (z + 1) % NZ, y, c), at(x, (z + NZ - 1) % NZ, y, c)
    sibling = at(x, z, y, 1 - c)
    partner = at(x, z, (1 - yh) * 2 + yl, 1 - c)

    barrier = pltpu.get_barrier_semaphore()

    def greet_plane(i, _):
        dx, dy, dc = i // 8, (i // 2) % 4, i % 2
        pl.semaphore_signal(
            barrier, inc=1, device_id=at((x + dx) % 4, z, (y + dy) % 4, (c + dc) % 2), device_id_type=MESH
        )
        return 0

    def greet_line(i, _):
        dz, dh = i // 2, i % 2
        pl.semaphore_signal(
            barrier, inc=1, device_id={"dp": ((z + dz) % NZ) * 2 + (yh + dh) % 2}, device_id_type=MESH
        )
        return 0

    lax.fori_loop(1, 32, greet_plane, 0)
    lax.fori_loop(2, 32, greet_line, 0)

    trow, tcol = trow_ref[...], tcol_ref[...]
    before = lax.broadcasted_iota(jnp.int32, (ROWS, ROWS), 0) < lax.broadcasted_iota(jnp.int32, (ROWS, ROWS), 1)
    same = jnp.where(jnp.logical_and(before, tcol == trow), 1.0, 0.0)
    slot = trow * SLOT + jnp.sum(same, axis=0, keepdims=True).astype(jnp.int32)
    pick[...] = jnp.where(
        lax.broadcasted_iota(jnp.int32, (32 * SLOT, ROWS), 0) == slot, 1.0, 0.0
    ).astype(jnp.bfloat16)

    pl.semaphore_wait(barrier, 61)

    own = z * 2 + c

    def chunk(m, s, ch):
        return weights.at[m, s, pl.ds(ch * CHUNK, CHUNK)]

    def swap_copy(m):
        return remote(w_ref.at[m], weights.at[m, z * 2 + 1 - c], swap_send.at[m], swap_recv.at[m], partner)

    def up_copy(m, zz, ch):
        return remote(
            chunk(m, zz * 2 + c, ch), chunk(m, zz * 2 + c, ch), ring_up_send.at[m, zz, ch], ring_recv.at[m, zz, ch], up
        )

    def down_copy(m, zz, ch):
        return remote(
            chunk(m, zz * 2 + c, ch), chunk(m, zz * 2 + c, ch), ring_down_send.at[m, zz, ch], ring_recv.at[m, zz, ch], down
        )

    def sib_copy(m, zz, cc):
        return remote(
            weights.at[m, zz * 2 + cc], weights.at[m, zz * 2 + cc], sib_send.at[m, zz], sib_recv.at[m, zz], sibling
        )

    def swap_start():
        @pl.when(yh != c)
        def _():
            for m in range(4):
                swap_copy(m).start()

        @pl.when(yh == c)
        def _():
            for m in range(4):
                weights[m, own] = w_ref[m]

    def ring_start(m):
        @pl.when(yh != c)
        def _():
            swap_copy(m).wait_recv()

        for ch in range(CHUNKS):
            up_copy(m, z, ch).start()
            down_copy(m, z, ch).start()
        sib_copy(m, z, c).start()

    def ring_tick(m, s):
        a, b = (z + NZ - s) % NZ, (z + s) % NZ
        for ch in range(CHUNKS):
            up_copy(m, a, ch).wait_recv()

            @pl.when((s < 7) | ((s == 7) & (ch == 0)))
            def _(ch=ch):
                up_copy(m, a, ch).start()

            @pl.when(s < 8)
            def _(ch=ch):
                down_copy(m, b, ch).wait_recv()

            @pl.when((s < 7) | ((s == 7) & (ch == 1)))
            def _(ch=ch):
                down_copy(m, b, ch).start()

        sib_copy(m, a, c).start()

        @pl.when(s < 8)
        def _():
            sib_copy(m, b, c).start()

    def ticks(low, high, work=None):
        def body(t, _):
            for m in range(4):
                s = t - STAGGER * m

                if low - STAGGER * m > 8 or high - STAGGER * m < 1:
                    continue

                @pl.when((s >= 1) & (s <= 8))
                def _(m=m, s=s):
                    ring_tick(m, s)

                if m < 3:

                    @pl.when(t == STAGGER * (m + 1))
                    def _(m=m):
                        ring_start(m + 1)

            if work is not None:
                work(t)
            return 0

        lax.fori_loop(low, high + 1, body, 0)

    def gather_copy(layer, i, g):
        dx, dy = i // 4, i % 4
        return remote(
            mine.at[layer], xs.at[layer, g], gather_send.at[layer, i], gather_recv.at[layer, g],
            at((x + dx) % 4, z, (y + dy) % 4, yh),
        )

    def gather_start(layer):
        def body(i, _):
            gather_copy(layer, i, group).start()
            return 0

        lax.fori_loop(1, 16, body, 0)

        @pl.when(c != yh)
        def _():
            gather_copy(layer, 0, group).start()

        @pl.when(c == yh)
        def _():
            xs[layer, group] = mine[layer]

    def gather_wait(layer, g):
        @pl.when((g != group) | (yh != c))
        def _():
            gather_copy(layer, 1, g).wait_recv()

    def begin_up():
        acc[...] = jnp.zeros_like(acc)
        acc_rest[...] = jnp.zeros_like(acc_rest)
        squares[...] = jnp.zeros_like(squares)

    def up_unit(layer, zz):
        m = 2 * layer
        gather_wait(layer, zz)
        sib_copy(m, zz, 1 - c).wait_recv()
        main, rest = weight_tiles(weights[m, zz * 2], weights[m, zz * 2 + 1])
        rows = xs[layer, zz]
        acc[...] += dot(rows, main)
        acc_rest[...] += dot_nt(rows, rest)
        wide = rows.astype(jnp.float32)
        wide = wide * wide
        squares[...] += wide[:, :128] + wide[:, 128:]

    def end_up():
        scale = lax.rsqrt(jnp.sum(squares[...], axis=1, keepdims=True) * (1.0 / DV) + EPSILON)

        def act(v):
            v = v * scale
            return (0.5 * v * (1.0 + jnp.tanh(0.7978845608028654 * (v + 0.044715 * (v * v * v))))).astype(jnp.bfloat16)

        hid[...] = act(acc[...])
        hid_rest[...] = act(acc_rest[...])

    def one_copy(layer, zz, yy):
        return remote(
            staged.at[layer, zz], first_sum.at[layer, zz // 4, yy], one_send.at[layer, zz], one_recv.at[layer, zz // 4, yy],
            at(x, z, c * 2 + (zz // 2) % 2, zz % 2),
        )

    def to_self(zz):
        return (yh == c) & ((zz // 2) % 2 == yl) & (zz % 2 == c)

    def down_unit(layer, zz):
        m = 2 * layer + 1
        sib_copy(m, zz, 1 - c).wait_recv()
        main, rest = weight_tiles(weights[m, zz * 2], weights[m, zz * 2 + 1])
        part = (dot_nt(hid[...], main) + dot(hid_rest[...], rest)).astype(jnp.bfloat16)

        @pl.when(to_self(zz))
        def _():
            first_sum[layer, zz // 4, y] = part

        @pl.when(jnp.logical_not(to_self(zz)))
        def _():
            staged[layer, zz] = part
            one_copy(layer, zz, y).start()

    def two_copy(layer, xx, src):
        return remote(
            staged_sum.at[layer, xx], second_sum.at[layer, src], two_send.at[layer, xx], two_recv.at[layer, src],
            at(xx, z, y, c),
        )

    def collect(layer):
        def body(i, _):
            xx = (x + i) % 4
            total = None
            for yy in range(4):

                @pl.when((yy != y) | (yh != c))
                def _(yy=yy):
                    one_copy(layer, xx * 4, yy).wait_recv()

                part = first_sum[layer, xx, yy].astype(jnp.float32)
                total = part if total is None else total + part
            total = total.astype(jnp.bfloat16)

            @pl.when(xx == x)
            def _():
                second_sum[layer, x] = total

            @pl.when(xx != x)
            def _():
                staged_sum[layer, xx] = total
                two_copy(layer, xx, x).start()

            return 0

        lax.fori_loop(0, 4, body, 0)

    def own_total(layer):
        total = mine[layer].astype(jnp.float32)
        for xx in range(4):

            @pl.when(xx != x)
            def _(xx=xx):
                two_copy(layer, x, xx).wait_recv()

            total = total + second_sum[layer, xx].astype(jnp.float32)
        return total.astype(jnp.bfloat16)

    def units(run, low, high):
        def body(i, _):
            d = (i + 1) // 2
            run((z + jnp.where(i % 2 == 1, d, NZ - d)) % NZ)
            return 0

        lax.fori_loop(low, high, body, 0)

    swap_start()
    mine[0] = x_ref[...]
    ring_start(0)
    gather_start(0)
    begin_up()
    ticks(1, 7)
    ticks(8, 11, lambda t: units(functools.partial(up_unit, 0), (t - 8) * 4, (t - 8) * 4 + 4))
    end_up()
    ticks(12, 15, lambda t: units(functools.partial(down_unit, 0), (t - 12) * 4, (t - 12) * 4 + 4))
    begin_up()
    ticks(16, 17)
    collect(0)
    ticks(18, 18)
    mine[1] = own_total(0)
    gather_start(1)
    ticks(19, 26)
    units(functools.partial(up_unit, 1), 0, 16)
    end_up()
    units(functools.partial(down_unit, 1), 0, 16)
    collect(1)
    second = own_total(1)
    outbox[...] = dot(pick[...], second).astype(jnp.bfloat16).reshape(32, SLOT, LANES)

    def route_copy(d, s):
        return remote(outbox.at[d], inbox.at[s], route_send.at[d], route_recv.at[s], {"dp": d})

    def route_start(i, _):
        route_copy((dp + i) % 32, dp).start()
        return 0

    lax.fori_loop(1, 32, route_start, 0)
    inbox[dp] = outbox[dp]

    @pl.when(yh != c)
    def _():
        for m in range(4):
            swap_copy(m).wait_send()

    def drain_ring(i, _):
        m, s = i // 9, i % 9
        a, b = (z + NZ - s) % NZ, (z + s) % NZ
        for ch in range(CHUNKS):

            @pl.when((s < 7) | ((s == 7) & (ch == 0)))
            def _(ch=ch):
                up_copy(m, a, ch).wait_send()

            @pl.when((s < 7) | ((s == 7) & (ch == 1)))
            def _(ch=ch):
                down_copy(m, b, ch).wait_send()

        sib_copy(m, a, c).wait_send()

        @pl.when((s > 0) & (s < 8))
        def _():
            sib_copy(m, b, c).wait_send()

        return 0

    lax.fori_loop(0, 36, drain_ring, 0)
    for layer in range(2):

        def drain_gather(i, _, layer=layer):
            gather_copy(layer, i, group).wait_send()
            return 0

        lax.fori_loop(1, 16, drain_gather, 0)

        @pl.when(c != yh)
        def _(layer=layer):
            gather_copy(layer, 0, group).wait_send()

        def drain_one(zz, _, layer=layer):
            @pl.when(jnp.logical_not(to_self(zz)))
            def _():
                one_copy(layer, zz, y).wait_send()

            return 0

        lax.fori_loop(0, 16, drain_one, 0)

        def drain_two(i, _, layer=layer):
            two_copy(layer, (x + i) % 4, x).wait_send()
            return 0

        lax.fori_loop(1, 4, drain_two, 0)

    def route_wait(i, _):
        route_copy((dp + i) % 32, (dp + i) % 32).wait()
        return 0

    lax.fori_loop(1, 32, route_wait, 0)
    r = lax.broadcasted_iota(jnp.int32, (32 * CAP, 32 * SLOT), 0)
    q = lax.broadcasted_iota(jnp.int32, (32 * CAP, 32 * SLOT), 1)
    squeeze = jnp.where(((q & 15) < CAP) & (r == (q >> 4) * CAP + (q & 15)), 1.0, 0.0).astype(jnp.bfloat16)
    out_ref[...] = dot(squeeze, inbox[...].reshape(32 * SLOT, LANES)).astype(jnp.bfloat16)


def pack(w):
    main = jnp.pad(w[:, :384], ((0, 12), (0, 0))).reshape(112, 3, 128).transpose(1, 0, 2).reshape(336, 128)
    return jnp.concatenate([main, jnp.pad(w[:, 384:].T, ((0, 0), (0, 28)))], axis=0)


def on_device(patches, up_first, down_first, up_second, down_second, targets):
    rows = jnp.pad(patches.reshape(ROWS, 2, HALF), ((0, 0), (0, 0), (0, 28))).reshape(ROWS, LANES)
    packed = jnp.stack([pack(up_first), pack(down_first.T), pack(up_second), pack(down_second.T)])
    bf16, dma = jnp.bfloat16, pltpu.SemaphoreType.DMA
    vmem = pl.BlockSpec(memory_space=pltpu.VMEM)
    placed = pl.pallas_call(
        kernel,
        out_shape=jax.ShapeDtypeStruct((32 * CAP, LANES), bf16),
        in_specs=[vmem] * 4,
        out_specs=vmem,
        scratch_shapes=[
            pltpu.VMEM((4, 32, PACK, 128), bf16),
            pltpu.VMEM((2, 16, ROWS, LANES), bf16),
            pltpu.VMEM((ROWS, 384), jnp.float32),
            pltpu.VMEM((ROWS, 16), jnp.float32),
            pltpu.VMEM((ROWS, 128), jnp.float32),
            pltpu.VMEM((ROWS, 384), bf16),
            pltpu.VMEM((ROWS, 16), bf16),
            pltpu.VMEM((2, 16, ROWS, LANES), bf16),
            pltpu.VMEM((2, 4, 4, ROWS, LANES), bf16),
            pltpu.VMEM((2, 4, ROWS, LANES), bf16),
            pltpu.VMEM((2, 4, ROWS, LANES), bf16),
            pltpu.VMEM((2, ROWS, LANES), bf16),
            pltpu.VMEM((32 * SLOT, ROWS), bf16),
            pltpu.VMEM((32, SLOT, LANES), bf16),
            pltpu.VMEM((32, SLOT, LANES), bf16),
            dma((4,)), dma((4,)),
            dma((4, NZ, CHUNKS)), dma((4, NZ, CHUNKS)), dma((4, NZ, CHUNKS)),
            dma((4, NZ)), dma((4, NZ)),
            dma((2, 16)), dma((2, 16)),
            dma((2, 16)), dma((2, 4, 4)),
            dma((2, 4)), dma((2, 4)),
            dma((32,)), dma((32,)),
        ],
        compiler_params=pltpu.CompilerParams(
            collective_id=0, has_side_effects=True, vmem_limit_bytes=48 * 1024 * 1024
        ),
    )(rows, packed, targets.reshape(1, ROWS), targets)
    return placed.reshape(32 * CAP, 2, 128)[:, :, :HALF].reshape(32 * CAP, 2 * HALF)


def solution(mesh):
    in_specs = (
        P("dp", ("section", "mp")),
        P("dp", ("section", "mp")),
        P(("section", "mp"), "dp"),
        P("dp", ("section", "mp")),
        P(("section", "mp"), "dp"),
        P("dp", None),
    )
    return jax.shard_map(
        on_device, mesh=mesh, in_specs=in_specs, out_specs=P("dp", ("section", "mp")), check_vma=False
    )
```

time: 907 us -> 184 us (0.20)
  waiting for transfers between devices: 786 us -> 0 us
  Pallas kernels: 0 us -> 175 us
  local copies, waits for them, and re-layouts: 53.7 us -> 9.07 us
  blocking collectives: 31.8 us -> 0 us
  matrix products: 13.6 us -> 0 us
  between operations: 13.6 us -> 0.15 us
    all_gather x6 -> x0, waiting for transfers between devices: 643 us -> none  [the longest x2 292 us: encoder_layer(): lax.all_gather(down_weight, 'dp', axis=1, tiled=True)]
    pallas_call x0 -> x1, Pallas kernels: none -> 175 us  [on_device(): pl.pallas_call(kernel, out_shape=jax.ShapeDtypeStruct((32 * CAP, LANES),...]
    unnamed x10 -> x0, waiting for transfers between devices: 143 us -> none
    all_to_all x1 -> x0, blocking collectives: 31.8 us -> none  [send_rows(): lax.all_to_all(outbox.reshape(devices, capacity, rows.shape[1]), 'dp', sp...]
    unnamed x12, local copies, waits for them, and re-layouts: 30.4 us -> 4.03 us
    all_gather x4 -> x0, local copies, waits for them, and re-layouts: 14.6 us -> none  [the longest x2 7.31 us: encoder_layer(): lax.all_gather(up_weight, 'dp', axis=0, tiled=True)]
    dot_general x2 -> x0, matrix products: 13.6 us -> none  [encoder_layer(): jnp.dot(hidden, lax.all_gather(down_weight, 'dp', axis=1, tiled=True), pr...]
  transfers between devices with their start and end apart: 8 -> 0, of which waited for: 8 -> 0; matrix products, arithmetic and copies ran while one was open for 5% -> 0% of each run, Pallas kernels for 0% -> 0%
where the time goes in v1:
time: 184 us
  Pallas kernels  175 us (95%)
  local copies, waits for them, and re-layouts  9.07 us (5%)
    pallas_call x1, Pallas kernels, on_device(): pl.pallas_call(kernel, out_shape=jax.ShapeDtypeStruct((32 * CAP, LANES),...  175 us
    unnamed x12, local copies, waits for them, and re-layouts  4.03 us

profile of v1, /device:TPU:1, one launch (start us, length us, event | category | flops | bytes accessed | tf_op | source)
XLA Modules:
  0.0 183.9 jit_solution(1657972472098169332)
XLA Ops:
  0.0 0.9 slice.36
  0.9 0.1 copy.14
  1.1 0.7 slice_bitcast_fusion.1
  1.7 0.0 slice-start
  1.7 0.9 slice-done
  2.7 0.0 copy-start.1
  2.7 0.1 copy.13
  2.8 0.8 copy-done.1
  3.6 0.0 copy-start.3
  3.6 0.9 copy-done.3
  4.5 0.1 copy.16
  4.6 0.0 slice-start.1
  4.6 0.9 slice-done.1
  5.6 0.0 copy-start.2
  5.6 0.1 copy.15
  5.7 0.8 copy-done.2
  6.5 0.0 copy-start.4
  6.5 0.8 copy-done.4
  7.4 0.1 reshape.39
  7.5 0.1 pad.30
  7.6 0.0 copy-start
  7.6 0.7 copy-done
  8.3 0.1 copy.17.tcol_ref
  8.4 174.6 %shard_map.64 = bf16[384,256]{1,0:T(8,128)(2,1)S(1)} custom-call(bf16[192,256]{1,0:T(8,128)(2,1)S(1)} %bitcast.42, bf16[4,352,128]{2,1,0:T(8,128)(2,1)S(1)} %pad_maximum_fusion.w_ref, s32[1,192]{1,0:T(1,128)S(1)} %bitcast.43, s32[192,1]{1,0:T(8,128)S(1)} %copy.17.tcol_ref), custom_call_target="tpu_custom_call" | custom-call | tf_op jit(solution)/shard_map/pallas_call | solution.py:427
  183.0 0.2 copy.19
  183.2 0.7 reshape.51
  (13 shorter events, 0.2 us)
Async XLA Ops:
  1.7 0.9 slice-start
  2.7 0.9 copy-start.1
  3.6 0.9 copy-start.3
  4.6 0.9 slice-start.1
  5.6 0.9 copy-start.2
  6.5 0.9 copy-start.4
  7.6 0.7 copy-start

commit v2 on v1

v2 whole, which is shorter than its diff:
```python
import functools

import jax
import jax.numpy as jnp
from jax import lax
from jax.experimental import pallas as pl
from jax.experimental.pallas import tpu as pltpu
from jax.sharding import PartitionSpec as P

MESH = pl.DeviceIdType.MESH
EPSILON = 1e-06
DV = 3200
ROWS = 192
NZ = 16
HALF = 100
PACK = 320
CHUNKS = 2
CHUNK = PACK // CHUNKS
LANES = 256
OFFSETS = (0, 0, 4, 4)
LAST = 12
CAP = 12
SLOT = 16


def remote(src, dst, send, recv, device):
    return pltpu.make_async_remote_copy(
        src_ref=src, dst_ref=dst, send_sem=send, recv_sem=recv, device_id=device, device_id_type=MESH
    )


def one_hot(mask):
    return jnp.where(mask, 1.0, 0.0).astype(jnp.bfloat16)


def iota(shape, axis):
    return lax.broadcasted_iota(jnp.int32, shape, axis)


def pack(block):
    turned = dot_nt(one_hot(iota((HALF, HALF), 0) == iota((HALF, HALF), 1)), block[0:384])
    tiles = [turned[:, 128 * j : 128 * j + 128] for j in range(3)]
    ends = jnp.concatenate([tile[96:100] for tile in tiles] + [jnp.zeros((4, 128), jnp.float32)], axis=0)
    return jnp.concatenate([tile[0:96].astype(jnp.bfloat16) for tile in tiles] + [ends.astype(jnp.bfloat16)], axis=0)


def weight_tiles(first, second):
    gap = jnp.zeros((16, 384), jnp.bfloat16)

    def wide(block):
        ends = block[288:304].astype(jnp.float32)
        none = jnp.zeros((12, 128), jnp.float32)
        ends = [jnp.concatenate([ends[4 * j : 4 * j + 4], none], axis=0).astype(jnp.bfloat16) for j in range(3)]
        return [jnp.concatenate([block[96 * j : 96 * j + 96] for j in range(3)], axis=1), jnp.concatenate(ends, axis=1), gap]

    main = jnp.concatenate(wide(first) + wide(second), axis=0)
    rest = jnp.concatenate([first[304:320], second[304:320]], axis=1)
    return main, rest


def dot(a, b):
    return jnp.dot(a, b, preferred_element_type=jnp.float32)


def dot_nt(a, b):
    return lax.dot_general(a, b, (((1,), (1,)), ((), ())), preferred_element_type=jnp.float32)


def kernel(
    x_hbm, w0_hbm, w1_hbm, w2_hbm, w3_hbm, trow_ref, out_ref,
    x_ref, w_ref, packed, load_sem, weights, xs, acc, acc_rest, squares, hid, hid_rest, staged, first_sum, staged_sum, second_sum, mine,
    pick, squeeze, outbox, inbox,
    swap_send, swap_recv, ring_up_send, ring_down_send, ring_recv, sib_send, sib_recv,
    gather_send, gather_recv, pass_y_send, pass_x_send, one_send, one_recv, two_send, two_recv, route_send, route_recv,
):
    x, dp, mp = lax.axis_index("section"), lax.axis_index("dp"), lax.axis_index("mp")
    z, yh, yl, c = dp // 2, dp % 2, mp // 2, mp % 2
    y = yh * 2 + yl
    group = x * 4 + mp

    def at(xx, zz, yy, cc):
        return {"section": xx, "dp": zz * 2 + yy // 2, "mp": (yy % 2) * 2 + cc}

    up, down = at(x, (z + 1) % NZ, y, c), at(x, (z + NZ - 1) % NZ, y, c)
    sibling = at(x, z, y, 1 - c)
    lane_y, lane_c = c * 2 + yl, yh
    lane, lane_sibling = at(x, z, lane_y, lane_c), at(x, z, lane_y, 1 - lane_c)
    lane_up, lane_down = at(x, (z + 1) % NZ, lane_y, lane_c), at(x, (z + NZ - 1) % NZ, lane_y, lane_c)

    barrier = pltpu.get_barrier_semaphore()

    def greet_plane(i, _):
        dx, dy, dc = i // 8, (i // 2) % 4, i % 2
        pl.semaphore_signal(
            barrier, inc=1, device_id=at((x + dx) % 4, z, (y + dy) % 4, (c + dc) % 2), device_id_type=MESH
        )
        return 0

    lax.fori_loop(1, 32, greet_plane, 0)
    for device in (up, down, lane_up, lane_down):
        pl.semaphore_signal(barrier, inc=1, device_id=device, device_id_type=MESH)

    loads = [pltpu.make_async_copy(x_hbm, x_ref, load_sem.at[4])]
    loads += [
        pltpu.make_async_copy(ref, w_ref.at[m], load_sem.at[m]) for m, ref in enumerate((w0_hbm, w1_hbm, w2_hbm, w3_hbm))
    ]
    for load in loads:
        load.start()

    trow = trow_ref[...]
    named = jnp.where(iota((32, ROWS), 0) == trow, 1.0, 0.0)
    before = one_hot(iota((ROWS, ROWS), 0) < iota((ROWS, ROWS), 1))
    position = jnp.sum(named * dot(named.astype(jnp.bfloat16), before), axis=0, keepdims=True).astype(jnp.int32)
    pick[...] = one_hot(iota((32 * SLOT, ROWS), 0) == trow * SLOT + position)

    for m in range(4):
        loads[1 + m].wait()
        packed[m, 0:304] = pack(w_ref[m])
        packed[m, 304:320] = jnp.zeros((16, 128), jnp.bfloat16)
        packed[m, 304:320, 0:HALF] = w_ref[m, 384:400]
    loads[0].wait()
    widen = one_hot(iota((2 * HALF, LANES), 1) == iota((2 * HALF, LANES), 0) + jnp.where(iota((2 * HALF, LANES), 0) < HALF, 0, 28))
    mine[0] = dot(x_ref[...], widen).astype(jnp.bfloat16)

    pl.semaphore_wait(barrier, 35)

    def chunk(m, s, ch):
        return weights.at[m, s, pl.ds(ch * CHUNK, CHUNK)]

    def up_copy(m, zz, ch):
        return remote(
            chunk(m, zz * 2 + c, ch), chunk(m, zz * 2 + c, ch), ring_up_send.at[m, zz, ch], ring_recv.at[m, zz, ch], up
        )

    def down_copy(m, zz, ch):
        return remote(
            chunk(m, zz * 2 + c, ch), chunk(m, zz * 2 + c, ch), ring_down_send.at[m, zz, ch], ring_recv.at[m, zz, ch], down
        )

    def sib_copy(m, zz, cc):
        return remote(
            weights.at[m, zz * 2 + cc], weights.at[m, zz * 2 + cc], sib_send.at[m, zz], sib_recv.at[m, zz], sibling
        )

    def start_copies(m):
        slot = z * 2 + lane_c
        copies = []
        for ch in range(CHUNKS):
            src, dst = packed.at[m, pl.ds(ch * CHUNK, CHUNK)], chunk(m, slot, ch)
            copies.append(remote(src, dst, ring_up_send.at[m, z, ch], ring_recv.at[m, z, ch], lane_up))
            copies.append(remote(src, dst, ring_down_send.at[m, z, ch], ring_recv.at[m, z, ch], lane_down))
        copies.append(remote(packed.at[m], weights.at[m, slot], sib_send.at[m, z], sib_recv.at[m, z], lane_sibling))
        return copies

    def lane_copy(m):
        return remote(packed.at[m], weights.at[m, z * 2 + lane_c], swap_send.at[m], swap_recv.at[m], lane)

    def ring_start(m):
        for copy in start_copies(m):
            copy.start()

        @pl.when(yh != c)
        def _():
            lane_copy(m).start()

        @pl.when(yh == c)
        def _():
            weights[m, z * 2 + c] = packed[m]

    def weights_wait(m, zz):
        sib_copy(m, zz, 1 - c).wait_recv()

        @pl.when((zz == z) & (yh != c))
        def _():
            lane_copy(m).wait_recv()

    def ring_tick(m, s):
        a, b = (z + NZ - s) % NZ, (z + s) % NZ
        for ch in range(CHUNKS):
            up_copy(m, a, ch).wait_recv()

            @pl.when((s < 7) | ((s == 7) & (ch == 0)))
            def _(ch=ch):
                up_copy(m, a, ch).start()

            @pl.when(s < 8)
            def _(ch=ch):
                down_copy(m, b, ch).wait_recv()

            @pl.when((s < 7) | ((s == 7) & (ch == 1)))
            def _(ch=ch):
                down_copy(m, b, ch).start()

        sib_copy(m, a, c).start()

        @pl.when(s < 8)
        def _():
            sib_copy(m, b, c).start()

    def ticks(low, high, work=None):
        def body(t, _):
            for m in range(4):
                if OFFSETS[m] and low <= OFFSETS[m] + 1 <= high:

                    @pl.when(t == OFFSETS[m] + 1)
                    def _(m=m):
                        ring_start(m)

            for m in range(4):
                s = t - OFFSETS[m]
                if low - OFFSETS[m] > 8 or high - OFFSETS[m] < 1:
                    continue

                @pl.when((s >= 1) & (s <= 8))
                def _(m=m, s=s):
                    ring_tick(m, s)

            if work is not None:
                work(t)
            return 0

        lax.fori_loop(low, high + 1, body, 0)

    def gather_copy(layer, i):
        return remote(
            mine.at[layer], xs.at[layer, group], gather_send.at[layer, i], gather_recv.at[layer, group],
            at((x + i * (1 - c)) % 4, z, (y + i * c) % 4, yh),
        )

    def pass_y_copy(layer, i, j):
        g = ((x + i) % 4) * 4 + yl * 2
        return remote(
            xs.at[layer, g], xs.at[layer, g], pass_y_send.at[layer, i, j], gather_recv.at[layer, g], at(x, z, (y + j) % 4, c)
        )

    def pass_x_copy(layer, i, j):
        g = x * 4 + i * 2 + 1
        return remote(
            xs.at[layer, g], xs.at[layer, g], pass_x_send.at[layer, i, j], gather_recv.at[layer, g], at((x + j) % 4, z, y, c)
        )

    def arrive(layer, g):
        @pl.when((g != group) | (yh != c))
        def _():
            remote(xs.at[layer, g], xs.at[layer, g], gather_send.at[layer, 0], gather_recv.at[layer, g], sibling).wait_recv()

    def gather_start(layer):
        for i in range(1, 4):
            gather_copy(layer, i).start()

        @pl.when(c != yh)
        def _():
            gather_copy(layer, 0).start()

        @pl.when(c == yh)
        def _():
            xs[layer, group] = mine[layer]

    def gather_pass(layer):
        for i in range(4):

            @pl.when(c == yh)
            def _(i=i):
                arrive(layer, ((x + i) % 4) * 4 + yl * 2)
                for j in range(1, 4):
                    pass_y_copy(layer, i, j).start()

            if i < 2:
                arrive(layer, x * 4 + i * 2 + 1)
                for j in range(1, 4):
                    pass_x_copy(layer, i, j).start()

    def gather_wait(layer, g):
        passed_y = (yh == c) & (g % 2 == 0) & ((g // 2) % 2 == yl)
        passed_x = (g % 2 == 1) & (g // 4 == x)

        @pl.when(jnp.logical_not(passed_y | passed_x))
        def _():
            arrive(layer, g)

    def begin_up():
        acc[...] = jnp.zeros_like(acc)
        acc_rest[...] = jnp.zeros_like(acc_rest)
        squares[...] = jnp.zeros_like(squares)

    def up_unit(layer, zz):
        m = 2 * layer
        gather_wait(layer, zz)
        weights_wait(m, zz)
        main, rest = weight_tiles(weights[m, zz * 2], weights[m, zz * 2 + 1])
        rows = xs[layer, zz]
        acc[...] += dot(rows, main)
        acc_rest[...] += dot_nt(rows, rest)
        wide = rows.astype(jnp.float32)
        wide = wide * wide
        squares[...] += wide[:, :128] + wide[:, 128:]

    def end_up():
        scale = lax.rsqrt(jnp.sum(squares[...], axis=1, keepdims=True) * (1.0 / DV) + EPSILON)

        def act(v):
            v = v * scale
            return (0.5 * v * (1.0 + jnp.tanh(0.7978845608028654 * (v + 0.044715 * (v * v * v))))).astype(jnp.bfloat16)

        hid[...] = act(acc[...])
        hid_rest[...] = act(acc_rest[...])

    def one_copy(layer, g):
        gx, gy, gc = g // 4, (g // 2) % 2, g % 2
        return remote(
            staged.at[layer, g],
            first_sum.at[layer, (1 - gc) * (gx // 2) + gc * (2 + gy), (1 - gc) * y + gc * x],
            one_send.at[layer, g],
            one_recv.at[layer, (1 - gc) * (gx // 2) + gc * (2 + gy), (1 - gc) * y + gc * x],
            at((1 - gc) * x + gc * gx, z, (1 - gc) * (c * 2 + gy) + gc * y, (1 - gc) * (gx % 2) + gc * c),
        )

    def to_self(g):
        gx, gy, gc = g // 4, (g // 2) % 2, g % 2
        return ((gc == 0) & (c * 2 + gy == y) & (gx % 2 == c)) | ((gc == 1) & (gx == x))

    def down_unit(layer, zz):
        m = 2 * layer + 1
        weights_wait(m, zz)
        main, rest = weight_tiles(weights[m, zz * 2], weights[m, zz * 2 + 1])
        part = (dot_nt(hid[...], main) + dot(hid_rest[...], rest)).astype(jnp.bfloat16)

        gx, gy, gc = zz // 4, (zz // 2) % 2, zz % 2

        @pl.when(to_self(zz))
        def _():
            first_sum[layer, (1 - gc) * (gx // 2) + gc * (2 + gy), (1 - gc) * y + gc * x] = part

        @pl.when(jnp.logical_not(to_self(zz)))
        def _():
            staged[layer, zz] = part
            one_copy(layer, zz).start()

    def two_copy(layer, k):
        if k < 2:
            device, src = at(2 * k + c, z, y, 0), x
        else:
            device, src = at(x, z, c * 2 + k - 2, 1), y
        return remote(
            staged_sum.at[layer, k], second_sum.at[layer, src], two_send.at[layer, k], two_recv.at[layer, src], device
        )

    def two_self(k):
        return (2 * k + c == x) & (c == 0) if k < 2 else (y == c * 2 + k - 2) & (c == 1)

    def collect(layer):
        for k in (0, 2, 1, 3):
            total = None
            for src in range(4):

                @pl.when((src != y) | (yh != c) if k < 2 else src != x)
                def _(k=k, src=src):
                    remote(
                        staged.at[layer, 0], first_sum.at[layer, k, src], one_send.at[layer, 0], one_recv.at[layer, k, src], sibling
                    ).wait_recv()

                part = first_sum[layer, k, src].astype(jnp.float32)
                total = part if total is None else total + part
            total = total.astype(jnp.bfloat16)

            @pl.when(two_self(k))
            def _(k=k, total=total):
                second_sum[layer, x if k < 2 else y] = total

            @pl.when(jnp.logical_not(two_self(k)))
            def _(k=k, total=total):
                staged_sum[layer, k] = total
                two_copy(layer, k).start()

    def own_total(layer):
        total = mine[layer].astype(jnp.float32)
        for src in range(4):

            @pl.when(jnp.logical_not(((c == 0) & (src == x) & (x % 2 == 0)) | ((c == 1) & (src == y) & (yh == 1))))
            def _(src=src):
                remote(
                    staged_sum.at[layer, 0], second_sum.at[layer, src], two_send.at[layer, 0], two_recv.at[layer, src], sibling
                ).wait_recv()

            total = total + second_sum[layer, src].astype(jnp.float32)
        return total.astype(jnp.bfloat16)

    def groups(run):
        def body(i, _):
            run(((x + 1 + i // 4) % 4) * 4 + ((yl + i // 2) % 2) * 2 + i % 2)
            return 0

        lax.fori_loop(0, 16, body, 0)

    def units(run, low, high):
        def body(i, _):
            d = (i + 1) // 2
            run((z + jnp.where(i % 2 == 1, d, NZ - d)) % NZ)
            return 0

        lax.fori_loop(low, high, body, 0)

    for m in range(4):
        if OFFSETS[m] == 0:
            ring_start(m)
    gather_start(0)
    begin_up()
    r, q = iota((32 * CAP, 32 * SLOT), 0), iota((32 * CAP, 32 * SLOT), 1)
    squeeze[...] = one_hot(((q & 15) < CAP) & (r == (q >> 4) * CAP + (q & 15)))
    ticks(1, 2)
    gather_pass(0)
    ticks(3, 8)
    units(functools.partial(up_unit, 0), 0, 16)
    end_up()
    groups(functools.partial(down_unit, 0))
    begin_up()
    ticks(9, 10)
    collect(0)
    ticks(11, 11)
    mine[1] = own_total(0)
    gather_start(1)
    ticks(12, LAST)
    gather_pass(1)
    units(functools.partial(up_unit, 1), 0, 16)
    end_up()
    groups(functools.partial(down_unit, 1))
    collect(1)
    second = own_total(1)
    outbox[...] = dot(pick[...], second).astype(jnp.bfloat16).reshape(32, SLOT, LANES)

    def route_copy(d, s):
        return remote(outbox.at[d], inbox.at[s], route_send.at[d], route_recv.at[s], {"dp": d})

    def route_start(i, _):
        route_copy((dp + i) % 32, dp).start()
        return 0

    lax.fori_loop(1, 32, route_start, 0)
    inbox[dp] = outbox[dp]

    for m in range(4):
        for copy in start_copies(m):
            copy.wait_send()

    @pl.when(yh != c)
    def _():
        for m in range(4):
            lane_copy(m).wait_send()

    def drain_ring(i, _):
        m, s = i // 8, i % 8 + 1
        a, b = (z + NZ - s) % NZ, (z + s) % NZ
        for ch in range(CHUNKS):

            @pl.when((s < 7) | ((s == 7) & (ch == 0)))
            def _(ch=ch):
                up_copy(m, a, ch).wait_send()

            @pl.when((s < 7) | ((s == 7) & (ch == 1)))
            def _(ch=ch):
                down_copy(m, b, ch).wait_send()

        sib_copy(m, a, c).wait_send()

        @pl.when(s < 8)
        def _():
            sib_copy(m, b, c).wait_send()

        return 0

    lax.fori_loop(0, 32, drain_ring, 0)
    for layer in range(2):

        for i in range(1, 4):
            gather_copy(layer, i).wait_send()

        @pl.when(c != yh)
        def _(layer=layer):
            gather_copy(layer, 0).wait_send()

        @pl.when(c == yh)
        def _(layer=layer):
            for i in range(4):
                for j in range(1, 4):
                    pass_y_copy(layer, i, j).wait_send()

        for i in range(2):
            for j in range(1, 4):
                pass_x_copy(layer, i, j).wait_send()

        def drain_one(g, _, layer=layer):
            @pl.when(jnp.logical_not(to_self(g)))
            def _():
                one_copy(layer, g).wait_send()

            return 0

        lax.fori_loop(0, 16, drain_one, 0)

        for k in range(4):

            @pl.when(jnp.logical_not(two_self(k)))
            def _(layer=layer, k=k):
                two_copy(layer, k).wait_send()

    def route_wait(i, _):
        route_copy((dp + i) % 32, (dp + i) % 32).wait()
        return 0

    lax.fori_loop(1, 32, route_wait, 0)
    rows = dot(squeeze[...], inbox[...].reshape(32 * SLOT, LANES)).astype(jnp.bfloat16)
    f = iota((2 * HALF, LANES), 0)
    narrow = one_hot(iota((2 * HALF, LANES), 1) == f + jnp.where(f < HALF, 0, 28))
    out_ref[...] = dot_nt(narrow, rows).astype(jnp.bfloat16)


def on_device(patches, up_first, down_first, up_second, down_second, targets):
    bf16, dma = jnp.bfloat16, pltpu.SemaphoreType.DMA
    vmem, anywhere = pl.BlockSpec(memory_space=pltpu.VMEM), pl.BlockSpec(memory_space=pl.ANY)
    placed = pl.pallas_call(
        kernel,
        out_shape=jax.ShapeDtypeStruct((2 * HALF, 32 * CAP), bf16),
        in_specs=[anywhere] * 5 + [vmem],
        out_specs=vmem,
        scratch_shapes=[
            pltpu.VMEM((ROWS, 2 * HALF), bf16),
            pltpu.VMEM((4, 400, HALF), bf16),
            pltpu.VMEM((4, PACK, 128), bf16),
            dma((5,)),
            pltpu.VMEM((4, 32, PACK, 128), bf16),
            pltpu.VMEM((2, 16, ROWS, LANES), bf16),
            pltpu.VMEM((ROWS, 384), jnp.float32),
            pltpu.VMEM((ROWS, 16), jnp.float32),
            pltpu.VMEM((ROWS, 128), jnp.float32),
            pltpu.VMEM((ROWS, 384), bf16),
            pltpu.VMEM((ROWS, 16), bf16),
            pltpu.VMEM((2, 16, ROWS, LANES), bf16),
            pltpu.VMEM((2, 4, 4, ROWS, LANES), bf16),
            pltpu.VMEM((2, 4, ROWS, LANES), bf16),
            pltpu.VMEM((2, 4, ROWS, LANES), bf16),
            pltpu.VMEM((2, ROWS, LANES), bf16),
            pltpu.VMEM((32 * SLOT, ROWS), bf16),
            pltpu.VMEM((32 * CAP, 32 * SLOT), bf16),
            pltpu.VMEM((32, SLOT, LANES), bf16),
            pltpu.VMEM((32, SLOT, LANES), bf16),
            dma((4,)), dma((4,)),
            dma((4, NZ, CHUNKS)), dma((4, NZ, CHUNKS)), dma((4, NZ, CHUNKS)),
            dma((4, NZ)), dma((4, NZ)),
            dma((2, 4)), dma((2, 16)), dma((2, 4, 4)), dma((2, 2, 4)),
            dma((2, 16)), dma((2, 4, 4)),
            dma((2, 4)), dma((2, 4)),
            dma((32,)), dma((32,)),
        ],
        compiler_params=pltpu.CompilerParams(
            collective_id=0, has_side_effects=True, vmem_limit_bytes=60 * 1024 * 1024
        ),
    )(patches, up_first.T, down_first, up_second.T, down_second, targets.reshape(1, ROWS))
    return placed.T


def solution(mesh):
    in_specs = (
        P("dp", ("section", "mp")),
        P("dp", ("section", "mp")),
        P(("section", "mp"), "dp"),
        P("dp", ("section", "mp")),
        P(("section", "mp"), "dp"),
        P("dp", None),
    )
    return jax.shard_map(
        on_device, mesh=mesh, in_specs=in_specs, out_specs=P("dp", ("section", "mp")), check_vma=False
    )
```

time: 184 us -> 140 us (0.76)
  Pallas kernels: 175 us -> 138 us
  local copies, waits for them, and re-layouts: 9.07 us -> 1.59 us
    pallas_call x1, Pallas kernels: 175 us -> 138 us  [on_device(): pl.pallas_call(kernel, out_shape=jax.ShapeDtypeStruct((2 * HALF, 32 * CAP...]
    slice x7 -> x0, local copies, waits for them, and re-layouts: 2.71 us -> none  [the longest x6 2.69 us: pack(): w[:, :384]]
    unnamed x12 -> x1, local copies, waits for them, and re-layouts: 4.03 us -> 1.59 us
where the time goes in v2:
time: 140 us; the launch traced here: 139 us
  Pallas kernels  138 us (99%)
  local copies, waits for them, and re-layouts  1.59 us (1%)
    pallas_call x1, Pallas kernels, on_device(): pl.pallas_call(kernel, out_shape=jax.ShapeDtypeStruct((2 * HALF, 32 * CAP...  138 us

profile of v2, /device:TPU:1, one launch (start us, length us, event | category | flops | bytes accessed | tf_op | source)
XLA Modules:
  0.0 139.5 jit_solution(6829387081162576801)
XLA Ops:
  0.0 137.9 %shard_map.64 = bf16[200,384]{1,0:T(8,128)(2,1)} custom-call(bf16[192,200]{1,0:T(8,128)(2,1)} %x_hbm.1, bf16[400,100]{1,0:T(8,128)(2,1)} %bitcast.5, bf16[400,100]{1,0:T(8,128)(2,1)} %w1_hbm.1, bf16[400,100]{1,0:T(8,128)(2,1)} %bitcast.6, bf16[400,100]{1,0:T(8,128)(2,1)} %w3_hbm.1, s32[1,192]{1,0:T(1,128)} %bitcast.7), custom_call_target="tpu_custom_call" | custom-call | tf_op jit(solution)/shard_map/pallas_call | solution.py:520
  137.9 1.6 %copy.8 = bf16[384,200]{0,1:T(8,128)(2,1)} copy(bf16[384,200]{0,1:T(8,128)(2,1)} %bitcast.4) | data formatting | bytes 307200

commit v3 on v0

v3 whole, which is shorter than its diff:
```python
import functools

import jax
import jax.numpy as jnp
from jax import lax
from jax.experimental import pallas as pl
from jax.experimental.pallas import tpu as pltpu
from jax.sharding import PartitionSpec as P

MESH = pl.DeviceIdType.MESH
EPSILON = 1e-06
DV = 3200
ROWS = 192
NZ = 16
HALF = 100
PACK = 320
OFFSETS = (0, 0, 7, 7)
LAST = 15
CAP = 12
SLOT = 16


def remote(src, dst, send, recv, device):
    return pltpu.make_async_remote_copy(
        src_ref=src, dst_ref=dst, send_sem=send, recv_sem=recv, device_id=device, device_id_type=MESH
    )


def one_hot(mask):
    return jnp.where(mask, 1.0, 0.0).astype(jnp.bfloat16)


def iota(shape, axis):
    return lax.broadcasted_iota(jnp.int32, shape, axis)


def pack(block):
    turned = dot_nt(one_hot(iota((HALF, HALF), 0) == iota((HALF, HALF), 1)), block[0:384])
    tiles = [turned[:, 128 * j : 128 * j + 128] for j in range(3)]
    ends = jnp.concatenate([tile[96:100] for tile in tiles] + [jnp.zeros((4, 128), jnp.float32)], axis=0)
    return jnp.concatenate([tile[0:96].astype(jnp.bfloat16) for tile in tiles] + [ends.astype(jnp.bfloat16)], axis=0)


def weight_tiles(block):
    ends = block[288:304].astype(jnp.float32)
    none = jnp.zeros((12, 128), jnp.float32)
    ends = [jnp.concatenate([ends[4 * j : 4 * j + 4], none], axis=0).astype(jnp.bfloat16) for j in range(3)]
    rows = [jnp.concatenate([block[96 * j : 96 * j + 96] for j in range(3)], axis=1), jnp.concatenate(ends, axis=1)]
    return jnp.concatenate(rows + [jnp.zeros((16, 384), jnp.bfloat16)], axis=0), block[304:320]


def wrap(v, n):
    return jnp.where(v >= n, v - n, v)


def split(v):
    high = jnp.where(v >= 2, 1, 0)
    return high, v - 2 * high


def dot(a, b):
    return jnp.dot(a, b, preferred_element_type=jnp.float32)


def dot_nt(a, b):
    return lax.dot_general(a, b, (((1,), (1,)), ((), ())), preferred_element_type=jnp.float32)


def kernel(
    x_hbm, w0_hbm, w1_hbm, w2_hbm, w3_hbm, trow_ref, out_ref,
    x_ref, w_ref, packed, load_sem, weights, xs, acc, acc_rest, squares, hid, hid_rest, staged, first_sum, staged_sum, second_sum, mine,
    pick, squeeze, outbox, inbox,
    lane_send, lane_recv, ring_send, ring_recv, sib_send, sib_recv,
    gather_send, extra_send, pass_send, gather_recv, rest_recv, one_send, one_recv, two_send, two_recv, route_send, route_recv,
):
    x, dp, mp = lax.axis_index("section"), lax.axis_index("dp"), lax.axis_index("mp")
    z, yh, yl, c = dp // 2, dp % 2, mp // 2, mp % 2
    y = yh * 2 + yl
    group = x * 4 + mp

    def at(xx, zz, yy, cc):
        high, low = split(yy)
        return {"section": xx, "dp": zz * 2 + high, "mp": low * 2 + cc}

    above, below = wrap(z + 1, NZ), wrap(z + NZ - 1, NZ)
    up, down = at(x, above, y, c), at(x, below, y, c)
    sibling = at(x, z, y, 1 - c)
    lane_y, lane_c = c * 2 + yl, yh
    lane, lane_sibling = at(x, z, lane_y, lane_c), at(x, z, lane_y, 1 - lane_c)
    lane_up, lane_down = at(x, above, lane_y, lane_c), at(x, below, lane_y, lane_c)

    barrier = pltpu.get_barrier_semaphore()

    for i in range(1, 32):
        device = at(wrap(x + i // 8, 4), z, wrap(y + (i // 2) % 4, 4), wrap(c + i % 2, 2))
        pl.semaphore_signal(barrier, inc=1, device_id=device, device_id_type=MESH)
    for device in (up, down, lane_up, lane_down):
        pl.semaphore_signal(barrier, inc=1, device_id=device, device_id_type=MESH)

    loads = [pltpu.make_async_copy(x_hbm, x_ref, load_sem.at[4])]
    loads += [
        pltpu.make_async_copy(ref, w_ref.at[m], load_sem.at[m]) for m, ref in enumerate((w0_hbm, w1_hbm, w2_hbm, w3_hbm))
    ]
    for load in loads:
        load.start()

    def prepare(m):
        loads[1 + m].wait()
        packed[m, 0:304] = pack(w_ref[m])
        packed[m, 304:320] = jnp.zeros((16, 128), jnp.bfloat16)
        packed[m, 304:320, 0:HALF] = w_ref[m, 384:400]

    prepare(0)
    prepare(1)
    pl.semaphore_wait(barrier, 35)

    def landed(ref, sem):
        pltpu.make_async_copy(ref, ref, sem).wait()

    def slot(m, zz, cc):
        return weights.at[m, zz * 2 + cc]

    def up_copy(m, zz):
        return remote(slot(m, zz, c), slot(m, zz, c), ring_send, ring_recv.at[m, zz], up)

    def down_copy(m, zz):
        return remote(slot(m, zz, c), slot(m, zz, c), ring_send, ring_recv.at[m, zz], down)

    def sib_copy(m, zz):
        return remote(slot(m, zz, c), slot(m, zz, c), sib_send, sib_recv.at[m], sibling)

    def lane_copy(m):
        return remote(packed.at[m], slot(m, z, lane_c), lane_send, lane_recv.at[m], lane)

    def ring_start(m):
        for device in (lane_up, lane_down):
            remote(packed.at[m], slot(m, z, lane_c), ring_send, ring_recv.at[m, z], device).start()
        remote(packed.at[m], slot(m, z, lane_c), sib_send, sib_recv.at[m], lane_sibling).start()

        @pl.when(yh != c)
        def _():
            lane_copy(m).start()

        @pl.when(yh == c)
        def _():
            weights[m, z * 2 + c] = packed[m]

    def weights_wait(m):
        landed(weights.at[m, pl.ds(0, NZ)], sib_recv.at[m])

        @pl.when(yh != c)
        def _():
            landed(weights.at[m, 0], lane_recv.at[m])

    def ring_tick(m, s):
        a, b = wrap(z + NZ - s, NZ), wrap(z + s, NZ)
        up_copy(m, a).wait_recv()

        @pl.when((s < 7) | ((s == 7) & (m % 2 == 0)))
        def _():
            up_copy(m, a).start()

        @pl.when(s < 8)
        def _():
            down_copy(m, b).wait_recv()

        @pl.when((s < 7) | ((s == 7) & (m % 2 == 1)))
        def _():
            down_copy(m, b).start()

        sib_copy(m, a).start()

        @pl.when(s < 8)
        def _():
            sib_copy(m, b).start()

    def ticks(low, high, work=None):
        def body(t, _):
            for m in range(4):
                if OFFSETS[m] and low <= OFFSETS[m] + 1 <= high:

                    @pl.when(t == OFFSETS[m] + 1)
                    def _(m=m):
                        ring_start(m)

            for m in range(4):
                s = t - OFFSETS[m]
                if low - OFFSETS[m] > 8 or high - OFFSETS[m] < 1:
                    continue

                @pl.when((s >= 1) & (s <= 8))
                def _(m=m, s=s):
                    ring_tick(m, s)

            if work is not None:
                work(t)
            return 0

        lax.fori_loop(low, high + 1, body, 0)

    def gather_copy(part, i):
        return remote(
            mine.at[part], xs.at[part, group], gather_send if i else extra_send, gather_recv.at[part, (1 - c) * x + c * (4 + yl)],
            at(wrap(x + i * (1 - c), 4), z, wrap(y + i * c, 4), yh),
        )

    def pass_y_copy(part, i, j):
        g = wrap(x + i, 4) * 4 + yl * 2
        return remote(
            xs.at[part, g], xs.at[part, g], pass_send, rest_recv.at[part], at(x, z, wrap(y + j, 4), c)
        )

    def pass_x_copy(part, i, j):
        g = x * 4 + i * 2 + 1
        return remote(
            xs.at[part, g], xs.at[part, g], gather_send, rest_recv.at[part], at(wrap(x + j, 4), z, y, c)
        )

    def arrive(part, g, k):
        @pl.when((g != group) | (yh != c))
        def _():
            landed(xs.at[part, 0], gather_recv.at[part, k])

    def gather_start(part):
        for i in range(1, 4):
            gather_copy(part, i).start()

        @pl.when(c != yh)
        def _():
            gather_copy(part, 0).start()

        @pl.when(c == yh)
        def _():
            xs[part, group] = mine[part]

    def gather_pass(part):
        for i in range(4):

            @pl.when(c == yh)
            def _(i=i):
                arrive(part, wrap(x + i, 4) * 4 + yl * 2, wrap(x + i, 4))
                for j in range(1, 4):
                    pass_y_copy(part, i, j).start()

            if i < 2:
                arrive(part, x * 4 + i * 2 + 1, 4 + i)
                for j in range(1, 4):
                    pass_x_copy(part, i, j).start()

    def gather_rest(part):
        @pl.when(yh == c)
        def _():
            landed(xs.at[part, pl.ds(0, 10)], rest_recv.at[part])

        @pl.when(yh != c)
        def _():
            landed(xs.at[part, pl.ds(0, 14)], rest_recv.at[part])

    def begin_up():
        acc[...] = jnp.zeros_like(acc)
        acc_rest[...] = jnp.zeros_like(acc_rest)
        squares[...] = jnp.zeros_like(squares)

    def up_unit(layer, zz):
        m = 2 * layer
        first, second = weight_tiles(weights[m, zz * 2]), weight_tiles(weights[m, zz * 2 + 1])
        halves = xs[2 * layer, zz], xs[2 * layer + 1, zz]
        rows = jnp.concatenate(halves, axis=1)
        acc[...] += dot(rows, jnp.concatenate([first[0], second[0]], axis=0))
        acc_rest[...] += dot_nt(rows, jnp.concatenate([first[1], second[1]], axis=1))
        for half in halves:
            wide = half.astype(jnp.float32)
            squares[...] += wide * wide

    def end_up():
        scale = lax.rsqrt(jnp.sum(squares[...], axis=1, keepdims=True) * (1.0 / DV) + EPSILON)

        def act(v):
            v = v * scale
            return (0.5 * v * (1.0 + jnp.tanh(0.7978845608028654 * (v + 0.044715 * (v * v * v))))).astype(jnp.bfloat16)

        hid[...] = act(acc[...])
        hid_rest[...] = act(acc_rest[...])

    def one_place(gx, gy, gc):
        return (split(gx)[0], y) if gc == 0 else (2 + gy, x)

    def one_copy(part, gx, gy, gc):
        k, src = one_place(gx, gy, gc)
        return remote(
            staged.at[part, gx * 4 + gy * 2 + gc], first_sum.at[part, k, src], one_send, one_recv.at[part, k],
            at(x, z, c * 2 + gy, split(gx)[1]) if gc == 0 else at(gx, z, y, c),
        )

    def to_self(gx, gy, gc):
        return (c * 2 + gy == y) & (split(gx)[1] == c) if gc == 0 else gx == x

    def down_unit(part, gx, gy, gc):
        m, half = 2 * (part // 2) + 1, part % 2

        main, rest = weight_tiles(weights[m, (gx * 4 + gy * 2 + gc) * 2 + half])
        total = (dot_nt(hid[...], main) + dot(hid_rest[...], rest)).astype(jnp.bfloat16)

        @pl.when(to_self(gx, gy, gc))
        def _():
            k, src = one_place(gx, gy, gc)
            first_sum[part, k, src] = total

        @pl.when(jnp.logical_not(to_self(gx, gy, gc)))
        def _():
            staged[part, gx * 4 + gy * 2 + gc] = total
            one_copy(part, gx, gy, gc).start()

    def two_copy(part, k):
        if k < 2:
            device, src = at(2 * k + c, z, y, 0), x
        else:
            device, src = at(x, z, c * 2 + k - 2, 1), y
        return remote(
            staged_sum.at[part, k], second_sum.at[part, src], two_send, two_recv.at[part], device
        )

    def two_self(k):
        return (2 * k + c == x) & (c == 0) if k < 2 else (y == c * 2 + k - 2) & (c == 1)

    def collect(part):
        for k in (0, 2, 1, 3):
            if k < 2:

                @pl.when(yh == c)
                def _(k=k):
                    landed(first_sum.at[part, k, pl.ds(0, 3)], one_recv.at[part, k])

                @pl.when(yh != c)
                def _(k=k):
                    landed(first_sum.at[part, k], one_recv.at[part, k])
            else:
                landed(first_sum.at[part, k, pl.ds(0, 3)], one_recv.at[part, k])
            total = None
            for src in range(4):
                term = first_sum[part, k, src].astype(jnp.float32)
                total = term if total is None else total + term
            total = total.astype(jnp.bfloat16)

            @pl.when(two_self(k))
            def _(k=k, total=total):
                second_sum[part, x if k < 2 else y] = total

            @pl.when(jnp.logical_not(two_self(k)))
            def _(k=k, total=total):
                staged_sum[part, k] = total
                two_copy(part, k).start()

    def own_total(part):
        with_self = ((c == 0) & (split(x)[1] == 0)) | ((c == 1) & (yh == 1))

        @pl.when(with_self)
        def _():
            landed(second_sum.at[part, pl.ds(0, 3)], two_recv.at[part])

        @pl.when(jnp.logical_not(with_self))
        def _():
            landed(second_sum.at[part], two_recv.at[part])

        total = mine[part].astype(jnp.float32)
        for src in range(4):
            total = total + second_sum[part, src].astype(jnp.float32)
        return total.astype(jnp.bfloat16)

    def groups(run):
        def body(i, _):
            gx = wrap(x + i, 4)
            for j in range(4):
                run(gx, wrap(yl + j // 2, 2), j % 2)
            return 0

        lax.fori_loop(1, 5, body, 0)

    def units(run):
        def body(s, _):
            run(wrap(z + s, NZ))
            run(wrap(z + NZ - s, NZ))
            return 0

        run(z)
        lax.fori_loop(1, 8, body, 0)
        run(wrap(z + 8, NZ))

    def route_copy(half, d, s):
        return remote(
            outbox.at[half, d], inbox.at[half, s], route_send, route_recv.at[half], {"dp": d}
        )

    def route_start(half):
        outbox[half] = dot(pick[...], own_total(2 + half)).astype(jnp.bfloat16).reshape(32, SLOT, 128)

        def body(i, _):
            for far in (16 - i, 16 + i):
                d = wrap(dp + far, 32)
                route_copy(half, d, dp).start()
            return 0

        route_copy(half, wrap(dp + 16, 32), dp).start()
        lax.fori_loop(1, 16, body, 0)
        inbox[half, dp] = outbox[half, dp]

    ring_start(0)
    ring_start(1)
    loads[0].wait()
    rows = x_ref[...]
    for half in range(2):
        shape = (2 * HALF, 128)
        widen = one_hot((iota(shape, 0) == iota(shape, 1) + half * HALF) & (iota(shape, 1) < HALF))
        mine[half] = dot(rows, widen).astype(jnp.bfloat16)
        gather_start(half)
    prepare(2)
    prepare(3)
    begin_up()
    trow = trow_ref[...]
    named = jnp.where(iota((32, ROWS), 0) == trow, 1.0, 0.0)
    before = one_hot(iota((ROWS, ROWS), 0) < iota((ROWS, ROWS), 1))
    position = jnp.sum(named * dot(named.astype(jnp.bfloat16), before), axis=0, keepdims=True).astype(jnp.int32)
    pick[...] = one_hot(iota((32 * SLOT, ROWS), 0) == trow * SLOT + position)

    r, q = iota((32 * CAP, 32 * SLOT), 0), iota((32 * CAP, 32 * SLOT), 1)
    squeeze[...] = one_hot(((q & 15) < CAP) & (r == (q >> 4) * CAP + (q & 15)))
    ticks(1, 2)
    gather_pass(0)
    gather_pass(1)
    ticks(3, 8)
    gather_rest(0)
    gather_rest(1)
    weights_wait(0)
    units(functools.partial(up_unit, 0))
    end_up()
    weights_wait(1)
    groups(functools.partial(down_unit, 0))
    groups(functools.partial(down_unit, 1))
    begin_up()
    ticks(9, 10)
    collect(0)
    collect(1)
    ticks(11, 11)
    mine[2] = own_total(0)
    gather_start(2)
    mine[3] = own_total(1)
    gather_start(3)
    ticks(12, 12)
    gather_pass(2)
    gather_pass(3)
    ticks(13, LAST)
    gather_rest(2)
    gather_rest(3)
    weights_wait(2)
    units(functools.partial(up_unit, 1))
    end_up()
    weights_wait(3)
    groups(functools.partial(down_unit, 2))
    groups(functools.partial(down_unit, 3))
    collect(2)
    collect(3)
    route_start(0)
    route_start(1)

    for half in range(2):
        landed(inbox.at[half, pl.ds(0, 31)], route_recv.at[half])

    landed(weights.at[:, pl.ds(0, 15)], ring_send)
    landed(weights.at[:, pl.ds(0, 16)], sib_send)
    landed(xs.at[:, pl.ds(0, 9)], gather_send)

    @pl.when(yh != c)
    def _():
        landed(weights.at[0, pl.ds(0, 4)], lane_send)
        landed(xs.at[:, 0], extra_send)
        landed(xs.at[:, pl.ds(0, 14)], one_send)

    @pl.when(yh == c)
    def _():
        landed(xs.at[:, pl.ds(0, 12)], pass_send)
        landed(xs.at[:, pl.ds(0, 12)], one_send)

    two_at_home = ((c == 0) & (split(x)[1] == 0)) | ((c == 1) & (yh == 1))

    @pl.when(two_at_home)
    def _():
        landed(staged_sum.at[:, pl.ds(0, 3)], two_send)

    @pl.when(jnp.logical_not(two_at_home))
    def _():
        landed(staged_sum, two_send)

    landed(inbox.at[:, pl.ds(0, 31)], route_send)
    total = None
    for half in range(2):
        rows = dot(squeeze[...], inbox[half].reshape(32 * SLOT, 128)).astype(jnp.bfloat16)
        shape = (2 * HALF, 128)
        narrow = one_hot((iota(shape, 0) == iota(shape, 1) + half * HALF) & (iota(shape, 1) < HALF))
        term = dot_nt(narrow, rows)
        total = term if total is None else total + term
    out_ref[...] = total.astype(jnp.bfloat16)


def on_device(patches, up_first, down_first, up_second, down_second, targets):
    bf16, dma = jnp.bfloat16, pltpu.SemaphoreType.DMA
    vmem, anywhere = pl.BlockSpec(memory_space=pltpu.VMEM), pl.BlockSpec(memory_space=pl.ANY)
    placed = pl.pallas_call(
        kernel,
        out_shape=jax.ShapeDtypeStruct((2 * HALF, 32 * CAP), bf16),
        in_specs=[anywhere] * 5 + [vmem],
        out_specs=vmem,
        scratch_shapes=[
            pltpu.VMEM((ROWS, 2 * HALF), bf16),
            pltpu.VMEM((4, 400, HALF), bf16),
            pltpu.VMEM((4, PACK, 128), bf16),
            dma((5,)),
            pltpu.VMEM((4, 32, PACK, 128), bf16),
            pltpu.VMEM((4, 16, ROWS, 128), bf16),
            pltpu.VMEM((ROWS, 384), jnp.float32),
            pltpu.VMEM((ROWS, 16), jnp.float32),
            pltpu.VMEM((ROWS, 128), jnp.float32),
            pltpu.VMEM((ROWS, 384), bf16),
            pltpu.VMEM((ROWS, 16), bf16),
            pltpu.VMEM((4, 16, ROWS, 128), bf16),
            pltpu.VMEM((4, 4, 4, ROWS, 128), bf16),
            pltpu.VMEM((4, 4, ROWS, 128), bf16),
            pltpu.VMEM((4, 4, ROWS, 128), bf16),
            pltpu.VMEM((4, ROWS, 128), bf16),
            pltpu.VMEM((32 * SLOT, ROWS), bf16),
            pltpu.VMEM((32 * CAP, 32 * SLOT), bf16),
            pltpu.VMEM((2, 32, SLOT, 128), bf16),
            pltpu.VMEM((2, 32, SLOT, 128), bf16),
            dma(()), dma((4,)),
            dma(()), dma((4, NZ)),
            dma(()), dma((4,)),
            dma(()), dma(()), dma(()), dma((4, 6)), dma((4,)),
            dma(()), dma((4, 4)),
            dma(()), dma((4,)),
            dma(()), dma((2,)),
        ],
        compiler_params=pltpu.CompilerParams(
            collective_id=0, has_side_effects=True, vmem_limit_bytes=60 * 1024 * 1024
        ),
    )(patches, up_first.T, down_first, up_second.T, down_second, targets.reshape(1, ROWS))
    return placed.T


def solution(mesh):
    in_specs = (
        P("dp", ("section", "mp")),
        P("dp", ("section", "mp")),
        P(("section", "mp"), "dp"),
        P("dp", ("section", "mp")),
        P(("section", "mp"), "dp"),
        P("dp", None),
    )
    return jax.shard_map(
        on_device, mesh=mesh, in_specs=in_specs, out_specs=P("dp", ("section", "mp")), check_vma=False
    )
```

time: 907 us -> 125 us (0.14)
  waiting for transfers between devices: 786 us -> 0 us
  Pallas kernels: 0 us -> 123 us
  local copies, waits for them, and re-layouts: 53.7 us -> 1.59 us
  blocking collectives: 31.8 us -> 0 us
  matrix products: 13.6 us -> 0 us
  between operations: 13.6 us -> 0.01 us
    all_gather x6 -> x0, waiting for transfers between devices: 643 us -> none  [the longest x2 292 us: encoder_layer(): lax.all_gather(down_weight, 'dp', axis=1, tiled=True)]
    unnamed x10 -> x0, waiting for transfers between devices: 143 us -> none
    pallas_call x0 -> x1, Pallas kernels: none -> 123 us  [on_device(): pl.pallas_call(kernel, out_shape=jax.ShapeDtypeStruct((2 * HALF, 32 * CAP...]
    all_to_all x1 -> x0, blocking collectives: 31.8 us -> none  [send_rows(): lax.all_to_all(outbox.reshape(devices, capacity, rows.shape[1]), 'dp', sp...]
    unnamed x12 -> x1, local copies, waits for them, and re-layouts: 30.4 us -> 1.59 us
    all_gather x4 -> x0, local copies, waits for them, and re-layouts: 14.6 us -> none  [the longest x2 7.31 us: encoder_layer(): lax.all_gather(up_weight, 'dp', axis=0, tiled=True)]
    dot_general x2 -> x0, matrix products: 13.6 us -> none  [encoder_layer(): jnp.dot(hidden, lax.all_gather(down_weight, 'dp', axis=1, tiled=True), pr...]
  transfers between devices with their start and end apart: 8 -> 0, of which waited for: 8 -> 0; matrix products, arithmetic and copies ran while one was open for 5% -> 0% of each run, Pallas kernels for 0% -> 0%
where the time goes in v3:
time: 125 us; the launch traced here: 124 us
  Pallas kernels  123 us (98%)
  local copies, waits for them, and re-layouts  1.59 us (1%)
    pallas_call x1, Pallas kernels, on_device(): pl.pallas_call(kernel, out_shape=jax.ShapeDtypeStruct((2 * HALF, 32 * CAP...  123 us

profile of v3, /device:TPU:1, one launch (start us, length us, event | category | flops | bytes accessed | tf_op | source)
XLA Modules:
  0.0 124.4 jit_solution(12734410584890155659)
XLA Ops:
  0.0 122.8 %shard_map.64 = bf16[200,384]{1,0:T(8,128)(2,1)} custom-call(bf16[192,200]{1,0:T(8,128)(2,1)} %x_hbm.1, bf16[400,100]{1,0:T(8,128)(2,1)} %bitcast.5, bf16[400,100]{1,0:T(8,128)(2,1)} %w1_hbm.1, bf16[400,100]{1,0:T(8,128)(2,1)} %bitcast.6, bf16[400,100]{1,0:T(8,128)(2,1)} %w3_hbm.1, s32[1,192]{1,0:T(1,128)} %bitcast.7), custom_call_target="tpu_custom_call" | custom-call | tf_op jit(solution)/shard_map/pallas_call | solution.py:507
  122.8 1.6 %copy.8 = bf16[384,200]{0,1:T(8,128)(2,1)} copy(bf16[384,200]{0,1:T(8,128)(2,1)} %bitcast.4) | data formatting | bytes 307200

commit v4 on v3

--- a/solution.py
+++ b/solution.py
@@ -14,6 +14,8 @@
 NZ = 16
 HALF = 100
 PACK = 320
+CHUNKS = 2
+CHUNK = PACK // CHUNKS
 OFFSETS = (0, 0, 7, 7)
 LAST = 15
 CAP = 12
@@ -120,11 +122,14 @@
     def slot(m, zz, cc):
         return weights.at[m, zz * 2 + cc]
 
-    def up_copy(m, zz):
-        return remote(slot(m, zz, c), slot(m, zz, c), ring_send, ring_recv.at[m, zz], up)
-
-    def down_copy(m, zz):
-        return remote(slot(m, zz, c), slot(m, zz, c), ring_send, ring_recv.at[m, zz], down)
+    def piece(m, zz, cc, ch):
+        return weights.at[m, zz * 2 + cc, pl.ds(ch * CHUNK, CHUNK)]
+
+    def up_copy(m, zz, ch):
+        return remote(piece(m, zz, c, ch), piece(m, zz, c, ch), ring_send, ring_recv.at[m, zz, ch], up)
+
+    def down_copy(m, zz, ch):
+        return remote(piece(m, zz, c, ch), piece(m, zz, c, ch), ring_send, ring_recv.at[m, zz, ch], down)
 
     def sib_copy(m, zz):
         return remote(slot(m, zz, c), slot(m, zz, c), sib_send, sib_recv.at[m], sibling)
@@ -133,8 +138,10 @@
         return remote(packed.at[m], slot(m, z, lane_c), lane_send, lane_recv.at[m], lane)
 
     def ring_start(m):
-        for device in (lane_up, lane_down):
-            remote(packed.at[m], slot(m, z, lane_c), ring_send, ring_recv.at[m, z], device).start()
+        for ch in range(CHUNKS):
+            src = packed.at[m, pl.ds(ch * CHUNK, CHUNK)]
+            for device in (lane_up, lane_down):
+                remote(src, piece(m, z, lane_c, ch), ring_send, ring_recv.at[m, z, ch], device).start()
         remote(packed.at[m], slot(m, z, lane_c), sib_send, sib_recv.at[m], lane_sibling).start()
 
         @pl.when(yh != c)
@@ -154,36 +161,37 @@
 
     def ring_tick(m, s):
         a, b = wrap(z + NZ - s, NZ), wrap(z + s, NZ)
-        up_copy(m, a).wait_recv()
-
-        @pl.when((s < 7) | ((s == 7) & (m % 2 == 0)))
-        def _():
-            up_copy(m, a).start()
+        for ch in range(CHUNKS):
+            up_copy(m, a, ch).wait_recv()
+
+            @pl.when((s < 7) | ((s == 7) & (m % 2 == 0)))
+            def _(ch=ch):
+                up_copy(m, a, ch).start()
+
+            @pl.when(s < 8)
+            def _(ch=ch):
+                down_copy(m, b, ch).wait_recv()
+
+            @pl.when((s < 7) | ((s == 7) & (m % 2 == 1)))
+            def _(ch=ch):
+                down_copy(m, b, ch).start()
+
+        sib_copy(m, a).start()
 
         @pl.when(s < 8)
         def _():
-            down_copy(m, b).wait_recv()
-
-        @pl.when((s < 7) | ((s == 7) & (m % 2 == 1)))
-        def _():
-            down_copy(m, b).start()
-
-        sib_copy(m, a).start()
-
-        @pl.when(s < 8)
-        def _():
             sib_copy(m, b).start()
 
-    def ticks(low, high, work=None):
+    def ticks(low, high, which=range(4)):
         def body(t, _):
-            for m in range(4):
+            for m in which:
                 if OFFSETS[m] and low <= OFFSETS[m] + 1 <= high:
 
                     @pl.when(t == OFFSETS[m] + 1)
                     def _(m=m):
                         ring_start(m)
 
-            for m in range(4):
+            for m in which:
                 s = t - OFFSETS[m]
                 if low - OFFSETS[m] > 8 or high - OFFSETS[m] < 1:
                     continue
@@ -192,8 +200,6 @@
                 def _(m=m, s=s):
                     ring_tick(m, s)
 
-            if work is not None:
-                work(t)
             return 0
 
         lax.fori_loop(low, high + 1, body, 0)
@@ -462,9 +468,6 @@
     route_start(0)
     route_start(1)
 
-    for half in range(2):
-        landed(inbox.at[half, pl.ds(0, 31)], route_recv.at[half])
-
     landed(weights.at[:, pl.ds(0, 15)], ring_send)
     landed(weights.at[:, pl.ds(0, 16)], sib_send)
     landed(xs.at[:, pl.ds(0, 9)], gather_send)
@@ -490,15 +493,16 @@
     def _():
         landed(staged_sum, two_send)
 
-    landed(inbox.at[:, pl.ds(0, 31)], route_send)
     total = None
     for half in range(2):
+        landed(inbox.at[half, pl.ds(0, 31)], route_recv.at[half])
         rows = dot(squeeze[...], inbox[half].reshape(32 * SLOT, 128)).astype(jnp.bfloat16)
         shape = (2 * HALF, 128)
         narrow = one_hot((iota(shape, 0) == iota(shape, 1) + half * HALF) & (iota(shape, 1) < HALF))
         term = dot_nt(narrow, rows)
         total = term if total is None else total + term
     out_ref[...] = total.astype(jnp.bfloat16)
+    landed(inbox.at[:, pl.ds(0, 31)], route_send)
 
 
 def on_device(patches, up_first, down_first, up_second, down_second, targets):
@@ -531,7 +535,7 @@
             pltpu.VMEM((2, 32, SLOT, 128), bf16),
             pltpu.VMEM((2, 32, SLOT, 128), bf16),
             dma(()), dma((4,)),
-            dma(()), dma((4, NZ)),
+            dma(()), dma((4, NZ, CHUNKS)),
             dma(()), dma((4,)),
             dma(()), dma(()), dma(()), dma((4, 6)), dma((4,)),
             dma(()), dma((4, 4)),

time: 125 us -> 121 us (0.968)
  Pallas kernels: 123 us -> 119 us
    pallas_call x1, Pallas kernels: 123 us -> 119 us  [on_device(): pl.pallas_call(kernel, out_shape=jax.ShapeDtypeStruct((2 * HALF, 32 * CAP...]
where the time goes in v4:
time: 121 us
  Pallas kernels  119 us (98%)
  local copies, waits for them, and re-layouts  1.59 us (1%)
    pallas_call x1, Pallas kernels, on_device(): pl.pallas_call(kernel, out_shape=jax.ShapeDtypeStruct((2 * HALF, 32 * CAP...  119 us

profile of v4, /device:TPU:1, one launch (start us, length us, event | category | flops | bytes accessed | tf_op | source)
XLA Modules:
  0.0 120.7 jit_solution(10431518779740279949)
XLA Ops:
  0.0 119.1 %shard_map.64 = bf16[200,384]{1,0:T(8,128)(2,1)} custom-call(bf16[192,200]{1,0:T(8,128)(2,1)} %x_hbm.1, bf16[400,100]{1,0:T(8,128)(2,1)} %bitcast.5, bf16[400,100]{1,0:T(8,128)(2,1)} %w1_hbm.1, bf16[400,100]{1,0:T(8,128)(2,1)} %bitcast.6, bf16[400,100]{1,0:T(8,128)(2,1)} %w3_hbm.1, s32[1,192]{1,0:T(1,128)} %bitcast.7), custom_call_target="tpu_custom_call" | custom-call | tf_op jit(solution)/shard_map/pallas_call | solution.py:511
  119.1 1.6 %copy.8 = bf16[384,200]{0,1:T(8,128)(2,1)} copy(bf16[384,200]{0,1:T(8,128)(2,1)} %bitcast.4) | data formatting | bytes 307200

commit v5 on v4

--- a/solution.py
+++ b/solution.py
@@ -176,11 +176,12 @@
             def _(ch=ch):
                 down_copy(m, b, ch).start()
 
-        sib_copy(m, a).start()
+    def sib_tick(m, s):
+        sib_copy(m, wrap(z + NZ - s, NZ)).start()
 
         @pl.when(s < 8)
         def _():
-            sib_copy(m, b).start()
+            sib_copy(m, wrap(z + s, NZ)).start()
 
     def ticks(low, high, which=range(4)):
         def body(t, _):
@@ -191,14 +192,15 @@
                     def _(m=m):
                         ring_start(m)
 
-            for m in which:
-                s = t - OFFSETS[m]
-                if low - OFFSETS[m] > 8 or high - OFFSETS[m] < 1:
-                    continue
-
-                @pl.when((s >= 1) & (s <= 8))
-                def _(m=m, s=s):
-                    ring_tick(m, s)
+            for step in (ring_tick, sib_tick):
+                for m in which:
+                    s = t - OFFSETS[m]
+                    if low - OFFSETS[m] > 8 or high - OFFSETS[m] < 1:
+                        continue
+
+                    @pl.when((s >= 1) & (s <= 8))
+                    def _(step=step, m=m, s=s):
+                        step(m, s)
 
             return 0
 

time: 121 us -> 127 us (1.050)
  Pallas kernels: 119 us -> 125 us
    pallas_call x1, Pallas kernels: 119 us -> 125 us  [on_device(): pl.pallas_call(kernel, out_shape=jax.ShapeDtypeStruct((2 * HALF, 32 * CAP...]
where the time goes in v5:
time: 127 us; the launch traced here: 126 us
  Pallas kernels  125 us (98%)
  local copies, waits for them, and re-layouts  1.59 us (1%)
    pallas_call x1, Pallas kernels, on_device(): pl.pallas_call(kernel, out_shape=jax.ShapeDtypeStruct((2 * HALF, 32 * CAP...  125 us

profile of v5, /device:TPU:1, one launch (start us, length us, event | category | flops | bytes accessed | tf_op | source)
XLA Modules:
  0.0 126.3 jit_solution(3229299199260853365)
XLA Ops:
  0.0 124.7 %shard_map.64 = bf16[200,384]{1,0:T(8,128)(2,1)} custom-call(bf16[192,200]{1,0:T(8,128)(2,1)} %x_hbm.1, bf16[400,100]{1,0:T(8,128)(2,1)} %bitcast.5, bf16[400,100]{1,0:T(8,128)(2,1)} %w1_hbm.1, bf16[400,100]{1,0:T(8,128)(2,1)} %bitcast.6, bf16[400,100]{1,0:T(8,128)(2,1)} %w3_hbm.1, s32[1,192]{1,0:T(1,128)} %bitcast.7), custom_call_target="tpu_custom_call" | custom-call | tf_op jit(solution)/shard_map/pallas_call | solution.py:513
  124.7 1.6 %copy.8 = bf16[384,200]{0,1:T(8,128)(2,1)} copy(bf16[384,200]{0,1:T(8,128)(2,1)} %bitcast.4) | data formatting | bytes 307200
